TPU v7x, 128 devices: a whole 4x4x4 slice. The times are simulated.
128 devices in a mesh: gx: 16 (over y, x), gy: 8 (over z, core).
Axes of the slice: x: 4, y: 4, z: 4, core: 2. Of those that a mesh axis runs over, the one named last changes fastest.
Arguments:
- inputs: bfloat16 [8192, 6144], P('gy', 'gx'), may hold values from -24 to 24, as said below
- preact: bfloat16 [8192, 24576], P('gy', 'gx'), may hold values from -6 to 6
- upstream: bfloat16 [8192, 24576], P('gy', 'gx'), as said below
- weight: float32 [6144, 24576], P('gy', 'gx'), may hold values from -72 to 72, as said below
- row_factor: float32 [6144], P('gy'), may hold values from 0.2 to 20, as said below
- column_factor: float32 [24576], P('gx'), may hold values from 0.5 to 5
Outputs:
- update: float32 [6144, 24576], P('gy', 'gx')
- new_row_factor: float32 [6144], P('gy')
- new_column_factor: float32 [24576], P('gx')
Inputs may be any that keep to these rules, and one draw needn't show every extreme that they name: `inputs`: entries lie within 24 in magnitude. `upstream`: entries lie within 36 / sqrt(8192) in magnitude. `weight`: entries lie within 72 in magnitude. `row_factor`: positive entries.
All inputs are finite; a program needn't handle non-finite values.
Results may differ from a plain program's by a relative error of at most 0.015.
Values may be sent and summed in bfloat16 or wider, within the bound.
No kernel may reach another device: no remote copies, remote signals or barrier semaphores. Data moves between devices by JAX's collectives and lax.ppermute only.
A program may use at most 192 MiB of HBM per device.

v0:
```python
import jax
import jax.numpy as jnp
from jax import lax
from jax.sharding import PartitionSpec as P

D = 6144
FF = 24576


second_decay = 0.8
clip_ratio = 1.0
unit_eps = 1e-06
factor_eps = 1e-30


def gelu_slope(preact, upstream):
    value = preact.astype(jnp.float32)
    normal_cdf = 0.5 * (1.0 + jax.scipy.special.erf(value * 0.7071067811865476))
    density = jnp.exp(-0.5 * value * value) * 0.3989422804014327
    return (upstream.astype(jnp.float32) * (normal_cdf + value * density)).astype(jnp.bfloat16)


def per_device(inputs, preact, upstream, weight, row_factor, column_factor):
    slope = gelu_slope(preact, upstream)
    features_all = lax.all_gather(inputs, "gx", axis=1, tiled=True)
    grad = lax.psum_scatter(
        lax.dot_general(
            features_all, slope, (((0,), (0,)), ((), ())), preferred_element_type=jnp.float32
        ).astype(jnp.bfloat16),
        "gy",
        scatter_dimension=0,
        tiled=True,
    ).astype(jnp.float32)
    weight_sq = weight * weight
    grad_local = jnp.sum(grad * grad, axis=0)
    weight_local = jnp.sum(weight_sq, axis=0)
    grad_sq, weight_col_sq = lax.psum((grad_local, weight_local), "gy")
    clip_factor = jnp.minimum(
        1.0, clip_ratio * jnp.sqrt(weight_col_sq) / (jnp.sqrt(grad_sq) + unit_eps)
    )
    clipped = grad * clip_factor[None, :]
    squared = clipped * clipped
    row_sums = lax.psum(jnp.sum(squared, axis=1), "gx")
    column_sums = lax.psum(jnp.sum(squared, axis=0), "gy")
    new_row = second_decay * row_factor + (1.0 - second_decay) * (row_sums / FF + factor_eps)
    new_column = second_decay * column_factor + (1.0 - second_decay) * (
        column_sums / D + factor_eps
    )
    row_mean = lax.psum(jnp.sum(new_row), "gy") / D
    weight_rms = jnp.sqrt(lax.psum(jnp.sum(weight_sq), ("gx", "gy")) / (D * FF))
    update = -weight_rms * clipped / jnp.sqrt(new_row[:, None] * new_column[None, :] / row_mean)
    return (update, new_row, new_column)


def solution(mesh):
    in_specs = (P("gy", "gx"), P("gy", "gx"), P("gy", "gx"), P("gy", "gx"), P("gy"), P("gx"))
    out_specs = (P("gy", "gx"), P("gy"), P("gx"))
    return jax.shard_map(
        per_device, mesh=mesh, in_specs=in_specs, out_specs=out_specs, check_vma=False
    )
```

profile of v0, /device:TPU:0, one launch (start us, length us, event | category | flops | bytes accessed | tf_op | source)
XLA Modules:
  0.0 345.2 jit_solution(17591232808871500145)
XLA Ops:
  7.2 0.0 all-gather.2.cloned.1.call-start
  7.2 0.7 all-gather.2.cloned.1.call-update
  7.9 0.0 reduce-scatter.2.cloned.1.call-start
  7.9 104.2 %all-gather.2.cloned.1.call-done = bf16[1024,6144]{1,0:T(8,128)(2,1)} async-done(((bf16[1024,384]{1,0:T(8,128)(2,1)}), bf16[1024,6144]{1,0:T(8,128)(2,1)}) %all-gather.2.cloned.1.call-update) | async-done | bytes 12582928 | tf_op jit(solution)/shard_map/all_gather | solution.py:25
  112.1 30.1 %fusion = bf16[6144,1536]{0,1:T(8,128)(2,1)} fusion(bf16[1024,6144]{1,0:T(8,128)(2,1)} %all-gather.2.cloned.1.call-done, bf16[1024,1536]{1,0:T(8,128)(2,1)} %param.7, bf16[1024,1536]{1,0:T(8,128)(2,1)} %param.8), kind=kOutput, calls=%fused_computation.1 | convolution fusion | flops 19355664384 | bytes 37748736 | tf_op jit(solution)/shard_map/dot_general | solution.py:27
  142.2 0.0 reduce-scatter.2.cloned.1.call-update
  142.2 0.0 copy-start.4
  142.2 0.0 copy-start.3
  142.2 4.2 %multiply_reduce_fusion.1 = (f32[]{:T(128)}, f32[1536]{0:T(1024)S(1)}) fusion(f32[768,1536]{1,0:T(8,128)} %param.9), kind=kLoop, calls=%fused_computation.23 | loop fusion | flops 3537407 | bytes 4724740 | tf_op jit(solution)/shard_map/reduce_sum | solution.py:50
  146.4 66.3 %psum.42 = f32[]{:T(128)} all-reduce(f32[]{:T(128)} %get-tuple-element.6), channel_id=1, replica_groups=mesh['gx'=16,'gy'=8] {'gx','gy'}, use_global_device_ids=true, to_apply=%region_1.0 | all-reduce | flops 1 | bytes 8 | tf_op jit(solution)/shard_map/psum | solution.py:50
  213.4 32.4 %reduce-scatter.2.cloned.1.call-done = bf16[768,1536]{0,1:T(8,128)(2,1)} async-done(((bf16[6144,1536]{0,1:T(8,128)(2,1)}), bf16[768,1536]{0,1:T(8,128)(2,1)}) %reduce-scatter.2.cloned.1.call-update) | async-done | bytes 2359312 | tf_op jit(solution)/shard_map/reduce_scatter | solution.py:26
  245.7 0.0 copy-start
  245.7 2.3 fusion.14
  248.1 23.6 %all-reduce.1 = (f32[1536]{0:T(1024)S(1)}, f32[1536]{0:T(1024)S(1)}) all-reduce(f32[1536]{0:T(1024)S(1)} %fusion.14, f32[1536]{0:T(1024)S(1)} %get-tuple-element.7), channel_id=1, replica_groups=mesh['gx'=16,'gy'=8] {'gy'}, use_global_device_ids=true, to_apply=%region_6.0 | all-reduce | flops 3072 | bytes 24576 | tf_op jit(solution)/shard_map/psum | solution.py:37
  271.7 2.6 fusion.11
  274.3 40.3 %psum.45 = f32[768]{0:T(1024)S(1)} all-reduce(f32[768]{0:T(1024)S(1)} %get-tuple-element.9), channel_id=1, replica_groups=mesh['gx'=16,'gy'=8] {'gx'}, use_global_device_ids=true, to_apply=%region_8.0 | all-reduce | flops 768 | bytes 6144 | tf_op jit(solution)/shard_map/psum | solution.py:43
  314.6 0.0 copy-done.4
  314.6 0.6 fusion.26
  315.2 0.0 copy-start.2
  315.2 13.5 %all-reduce = (f32[]{:T(128)}, f32[1536]{0:T(1024)S(1)}) all-reduce(f32[]{:T(128)} %get-tuple-element.14, f32[1536]{0:T(1024)S(1)} %get-tuple-element.8), channel_id=1, replica_groups=mesh['gx'=16,'gy'=8] {'gy'}, use_global_device_ids=true, to_apply=%region_12.0 | all-reduce | flops 1537 | bytes 12296 | tf_op jit(solution)/shard_map/psum | solution.py:49
  328.7 0.0 copy-done.3
  328.7 0.0 copy-start.1
  329.4 0.0 copy-done
  329.4 2.9 fusion.13
  332.4 6.0 %copy.9 = f32[768,1536]{1,0:T(8,128)} copy(f32[768,1536]{0,1:T(8,128)} %fusion.13) | data formatting | bytes 9437184
  338.4 0.0 copy-done.2
  338.4 0.0 copy-done.1
  (2 shorter events, 0.0 us)
Async XLA Ops:
  7.2 105.0 %all-gather.2.cloned.1.call-start = ((), (), s32[]{:S(2)}) async-start(), calls=%async_computation.1 | async-start | bytes 13369344 | tf_op jit(solution)/shard_map/all_gather | solution.py:25
  7.9 237.8 %reduce-scatter.2.cloned.1.call-start = ((), (), s32[]{:S(2)}) async-start(), calls=%async_computation.2 | async-start | bytes 21233664 | tf_op jit(solution)/shard_map/reduce_scatter | solution.py:26
  142.2 172.4 %copy-start.4 = (f32[768]{0:T(1024)S(1)}, f32[768]{0:T(1024)}, u32[]{:S(2)}) copy-start(f32[768]{0:T(1024)} %param.10) | copy-start | bytes 9220
  142.2 186.5 %copy-start.3 = (f32[1536]{0:T(1024)S(1)}, f32[1536]{0:T(1024)}, u32[]{:S(2)}) copy-start(f32[1536]{0:T(1024)} %param.11) | copy-start | bytes 18436
  245.7 83.7 %copy-start = (bf16[768,1536]{0,1:T(8,128)(2,1)S(1)}, bf16[768,1536]{0,1:T(8,128)(2,1)}, u32[]{:S(2)}) copy-start(bf16[768,1536]{0,1:T(8,128)(2,1)} %reduce-scatter.2.cloned.1.call-done) | copy-start | bytes 7077892
  315.2 23.2 %copy-start.2 = (f32[768]{0:T(1024)}, f32[768]{0:T(1024)S(1)}, u32[]{:S(2)}) copy-start(f32[768]{0:T(1024)S(1)} %get-tuple-element.15) | copy-start | bytes 9220
  328.7 9.7 %copy-start.1 = (f32[1536]{0:T(1024)}, f32[1536]{0:T(1024)S(1)}, u32[]{:S(2)}) copy-start(f32[1536]{0:T(1024)S(1)} %multiply_add_fusion) | copy-start | bytes 18436
Sparse Core Ops, SparseCore 0:
  10.1 101.9 all-gather.1
  142.3 103.3 reduce-scatter.1
where the time goes:
time: 346 us; the launch traced here: 345 us
  blocking collectives  144 us (42%)
  waiting for transfers between devices  137 us (40%)
  matrix products  30.1 us (9%)
  between operations  15.4 us (4%)
  other arithmetic  12.7 us (4%)
  local copies, waits for them, and re-layouts  6.07 us (2%)
    all_gather x1, waiting for transfers between devices, per_device(): features_all = lax.all_gather(inputs, 'gx', axis=1, tiled=True)  104 us
    psum x1, blocking collectives, per_device(): weight_rms = jnp.sqrt(lax.psum(jnp.sum(weight_sq), ('gx', 'gy')) / (D * FF))  66.3 us
    psum x1, blocking collectives, per_device(): row_sums = lax.psum(jnp.sum(squared, axis=1), 'gx')  40.3 us
    reduce_scatter x1, waiting for transfers between devices, per_device(): lax.psum_scatter(lax.dot_general(features_all, slope, (((0,), (0,)), ((),...  32.4 us
    dot_general x1, matrix products, per_device(): lax.dot_general(features_all, slope, (((0,), (0,)), ((), ())), preferred_...  30.1 us
    psum x1, blocking collectives, per_device(): grad_sq, weight_col_sq = lax.psum((grad_local, weight_local), 'gy')  23.6 us
    psum x1, blocking collectives, per_device(): row_mean = lax.psum(jnp.sum(new_row), 'gy') / D  13.5 us
  transfers between devices with their start and end apart: 2, of which 2 were waited for; matrix products, arithmetic and copies ran while one was open for 1% of the time, Pallas kernels for 0%

commit v1 on v0

v1 whole, which is shorter than its diff:
```python
import jax
import jax.numpy as jnp
from jax import lax
from jax.experimental import pallas as pl
from jax.experimental.pallas import tpu as pltpu
from jax.sharding import PartitionSpec as P

D = 6144
FF = 24576
TOK = 1024
FEAT = 384
HALF = 768
NCH = 2

second_decay = 0.8
clip_ratio = 1.0
unit_eps = 1e-06
factor_eps = 1e-30

BOTH = ("gx", "gy")
FLIP = (0, 2, 1, 3)


def moves(dx, dy, dz, other_core):
    pairs = []
    for y in range(4):
        for x in range(4):
            for z in range(4):
                for core in range(2):
                    s = 1 - 2 * core
                    tx, ty, tz = (x + s * dx) % 4, (y + s * dy) % 4, (z + s * dz) % 4
                    tc = 1 - core if other_core else core
                    pairs.append(((y * 4 + x) * 8 + z * 2 + core, (ty * 4 + tx) * 8 + tz * 2 + tc))
    return pairs


ALONG_X = moves(1, 0, 0, False)
ALONG_Y = moves(0, 1, 0, False)
ALONG_Z = moves(0, 0, 1, False)
SWAP = moves(0, 0, 0, True)


def send(value, pairs):
    return lax.ppermute(value, BOTH, pairs)


def gelu_slope(preact, upstream):
    value = preact.astype(jnp.float32)
    normal_cdf = 0.5 * (1.0 + jax.scipy.special.erf(value * 0.7071067811865476))
    density = jnp.exp(-0.5 * value * value) * 0.3989422804014327
    return (upstream.astype(jnp.float32) * (normal_cdf + value * density)).astype(jnp.bfloat16)


def gather_ring(own, other, pairs):
    behind_own = send(own, pairs)
    behind_other = send(other, pairs)
    opposite_own = send(behind_own, pairs)
    ahead_other = send(behind_own, SWAP)
    ahead_own = send(behind_other, SWAP)
    opposite_other = send(opposite_own, SWAP)
    return (behind_own, behind_other), (ahead_own, ahead_other), (opposite_own, opposite_other)


def unit_partials(order, slope_own, slope_other, entries):
    arrays = []
    position = {}
    plan = []
    rows = 0
    for places in entries:
        count = places[0][0][0].shape[-2]
        for i, halves in enumerate(places):
            for h, (array, index) in enumerate(halves):
                if id(array) not in position:
                    position[id(array)] = len(arrays)
                    arrays.append(array)
                plan.append((i, h, rows, count, position[id(array)], index))
        rows += count

    def kernel(order_ref, own_ref, other_ref, *refs):
        feature_refs = refs[: len(arrays)]
        out_last, out_1, out_2, out_3, held, sems = refs[len(arrays) :]
        for i, h, start, count, which, index in plan:
            source = feature_refs[which]
            source = source.at[index] if index is not None else source
            pltpu.make_async_copy(
                source, held.at[i, h, pl.ds(start, count)], sems.at[i]
            ).start()

        @pl.loop(0, 4)
        def _(i):
            pltpu.make_async_copy(held.at[i], held.at[i], sems.at[i]).wait()
            total = jnp.dot(held[i, 0], own_ref[...], preferred_element_type=jnp.float32)
            total += jnp.dot(held[i, 1], other_ref[...], preferred_element_type=jnp.float32)
            place = order_ref[i]

            @pl.when(place == 0)
            def _():
                out_last[...] = total

            for k, out in ((1, out_1), (2, out_2), (3, out_3)):

                @pl.when(place == k)
                def _():
                    out[...] = total.astype(jnp.bfloat16)

    narrow = jax.ShapeDtypeStruct((rows, HALF), jnp.bfloat16)
    vmem = pl.BlockSpec(memory_space=pltpu.VMEM)
    return pl.pallas_call(
        kernel,
        out_shape=(jax.ShapeDtypeStruct((rows, HALF), jnp.float32), narrow, narrow, narrow),
        in_specs=[pl.BlockSpec(memory_space=pltpu.SMEM), vmem, vmem]
        + [pl.BlockSpec(memory_space=pl.ANY)] * len(arrays),
        out_specs=(vmem,) * 4,
        scratch_shapes=[
            pltpu.VMEM((4, 2, rows, TOK), jnp.bfloat16),
            pltpu.SemaphoreType.DMA((4,)),
        ],
        compiler_params=pltpu.CompilerParams(vmem_limit_bytes=40 << 20),
        cost_estimate=pl.CostEstimate(
            flops=2 * 4 * rows * HALF * 2 * TOK,
            bytes_accessed=4 * rows * 2 * TOK * 2 + 2 * TOK * HALF * 2 + 10 * rows * HALF,
            transcendentals=0,
        ),
    )(order, slope_own, slope_other, *arrays)


def reduce_ring(order, slope_own, slope_other, entries):
    last, first, second, third = unit_partials(order, slope_own, slope_other, entries)
    got = send(first, ALONG_Z)
    got = send((second.astype(jnp.float32) + got.astype(jnp.float32)).astype(jnp.bfloat16), ALONG_Z)
    got = send((third.astype(jnp.float32) + got.astype(jnp.float32)).astype(jnp.bfloat16), ALONG_Z)
    return last + got.astype(jnp.float32)


def everyone(vector, axis, count):
    return lax.all_to_all(
        jnp.broadcast_to(vector[None, :], (count,) + vector.shape), axis, 0, 0, tiled=True
    )


def per_device(inputs, preact, upstream, weight, row_factor, column_factor):
    gx, gy = lax.axis_index("gx"), lax.axis_index("gy")
    y, x, z, core = gx // 4, gx % 4, gy // 2, gy % 2
    s = 1 - 2 * core
    steps = jnp.array([0, -1, 1, 2], jnp.int32)
    order = (s * (z - y) - steps) % 4

    features = inputs.T
    both = (features, send(features, SWAP))
    size = FEAT // 2 // NCH
    p_here = tuple(v[: FEAT // 2] for v in both)
    q_here = tuple(v[FEAT // 2 :] for v in both)

    def part(value, start):
        return lax.dynamic_slice_in_dim(value, start * HALF, HALF, 1)

    slope_mine = gelu_slope(part(preact, core), part(upstream, core))
    slope_yours = gelu_slope(part(preact, 1 - core), part(upstream, 1 - core))
    slope_other = send(slope_yours, SWAP)
    ring = lambda entries: reduce_ring(order, slope_mine, slope_other, entries)

    p_behind, p_ahead, p_opposite = gather_ring(*p_here, ALONG_Y)
    q_behind, q_ahead, q_opposite = gather_ring(*q_here, ALONG_X)
    p_all = [p_here, p_behind, p_ahead, p_opposite]
    q_all = [q_here, q_behind, q_ahead, q_opposite]

    pieces = []
    own_p = ring([[tuple((v[h], None) for h in range(2)) for v in p_all]])
    pieces.append([(0, 0, FEAT // 2, own_p)])
    for chunk in range(NCH):
        lo = chunk * size
        p_own, p_other = (jnp.stack([v[h][lo : lo + size] for v in p_all]) for h in range(2))
        q_own, q_other = (jnp.stack([v[h][lo : lo + size] for v in q_all]) for h in range(2))
        behind, ahead, opposite = gather_ring(p_own, p_other, ALONG_X)
        near = ring(
            [
                [((behind[0], i), (behind[1], i)) for i in range(4)],
                [((ahead[0], FLIP[i]), (ahead[1], FLIP[i])) for i in range(4)],
            ]
        )
        pieces.append([(1, lo, size, near[:size]), (2, lo, size, near[size:])])
        q_b, q_a, q_o = gather_ring(q_own, q_other, ALONG_Y)
        entries = [[((opposite[0], i), (opposite[1], FLIP[i])) for i in range(4)]]
        for g in range(4):
            entries.append(
                [
                    ((q_own, g), (q_other, g)),
                    ((q_b[0], g), (q_b[1], g)),
                    ((q_a[0], FLIP[g]), (q_a[1], FLIP[g])),
                    ((q_o[0], g), (q_o[1], FLIP[g])),
                ]
            )
        far = ring(entries)
        group = [(3, lo, size, far[:size])]
        for g in range(4):
            group.append((g, FEAT // 2 + lo, size, far[(g + 1) * size : (g + 2) * size]))
        pieces.append(group)

    places = {}
    for group in pieces:
        for g, start, _, value in group:
            places[(g, start)] = value
    grad_rel = jnp.stack(
        [jnp.concatenate([places[k] for k in sorted(places) if k[0] == g]) for g in range(4)]
    )

    weight_sq = weight * weight
    weight_local = jnp.sum(weight_sq, axis=0)
    grad_local = jnp.sum(grad_rel * grad_rel, axis=(0, 1))
    where = jnp.array([0, 2, 3, 1], jnp.int32)

    def rows_of(owner):
        out = []
        for i in range(2):
            at = where[(s * (2 * owner + i - x)) % 4]
            out.append(lax.dynamic_index_in_dim(grad_rel, at, 0, keepdims=False))
        return jnp.concatenate(out)

    kept = rows_of(core)
    got = send(rows_of(1 - core), SWAP)
    row_local = jnp.broadcast_to(jnp.sum(row_factor)[None], (128,))
    gathered = everyone(jnp.concatenate([grad_local, weight_local, row_local]), "gy", 8)
    grad_sq = jnp.sum(gathered[:, :HALF].reshape(4, 2 * HALF), axis=0)
    weight_col_sq = jnp.sum(gathered[:, HALF : 3 * HALF], axis=0)
    row_total = jnp.sum(gathered[:, 3 * HALF])

    clip_factor = jnp.minimum(
        1.0, clip_ratio * jnp.sqrt(weight_col_sq) / (jnp.sqrt(grad_sq) + unit_eps)
    )
    column_sums = clip_factor * clip_factor * grad_sq
    new_column = second_decay * column_factor + (1.0 - second_decay) * (
        column_sums / D + factor_eps
    )
    grad = jnp.concatenate(
        [jnp.where(core == 0, kept, got), jnp.where(core == 0, got, kept)], axis=1
    )
    clipped = grad * clip_factor[None, :]
    row_part = jnp.sum(clipped * clipped, axis=1)
    totals = jnp.concatenate(
        [
            jnp.broadcast_to(jnp.sum(column_sums)[None], (128,)),
            jnp.broadcast_to(jnp.sum(weight_col_sq)[None], (128,)),
        ]
    )
    summed = jnp.sum(everyone(jnp.concatenate([row_part, totals]), "gx", 16), axis=0)
    row_sums, clipped_total, weight_total = summed[:768], summed[768], summed[896]
    new_row = second_decay * row_factor + (1.0 - second_decay) * (row_sums / FF + factor_eps)
    row_mean = (
        second_decay * row_total + (1.0 - second_decay) * (clipped_total / FF + D * factor_eps)
    ) / D
    weight_rms = jnp.sqrt(weight_total / (D * FF))
    update = (
        -weight_rms
        * clipped
        * lax.rsqrt(new_row)[:, None]
        * (jnp.sqrt(row_mean) * lax.rsqrt(new_column))[None, :]
    )
    return (update, new_row, new_column)


def solution(mesh):
    in_specs = (P("gy", "gx"), P("gy", "gx"), P("gy", "gx"), P("gy", "gx"), P("gy"), P("gx"))
    out_specs = (P("gy", "gx"), P("gy"), P("gx"))
    return jax.shard_map(
        per_device, mesh=mesh, in_specs=in_specs, out_specs=out_specs, check_vma=False
    )
```

time: 346 us -> 269 us (0.78)
  blocking collectives: 144 us -> 0 us
  Pallas kernels: 0 us -> 56.7 us
  starting transfers between devices: 0.08 us -> 53.4 us
  waiting for transfers between devices: 137 us -> 97.8 us
  matrix products: 30.1 us -> 0 us
  other arithmetic: 12.7 us -> 28.7 us
  local copies, waits for them, and re-layouts: 6.07 us -> 20.4 us
  between operations: 15.4 us -> 11.2 us
    psum x4 -> x0, blocking collectives: 144 us -> none  [the longest x1 66.3 us: per_device(): weight_rms = jnp.sqrt(lax.psum(jnp.sum(weight_sq), ('gx', 'gy')) / (D * FF))]
    all_gather x1 -> x0, waiting for transfers between devices: 104 us -> none  [per_device(): features_all = lax.all_gather(inputs, 'gx', axis=1, tiled=True)]
    ppermute x0 -> x54, waiting for transfers between devices: none -> 85.7 us  [send(): return lax.ppermute(value, BOTH, pairs)]
    pallas_call x0 -> x5, Pallas kernels: none -> 56.7 us  [unit_partials(): pl.pallas_call(kernel, out_shape=(jax.ShapeDtypeStruct((rows, HALF), jnp....]
    ppermute x0 -> x54, starting transfers between devices: none -> 44.7 us  [send(): return lax.ppermute(value, BOTH, pairs)]
    reduce_scatter x1 -> x0, waiting for transfers between devices: 32.4 us -> none  [per_device(): lax.psum_scatter(lax.dot_general(features_all, slope, (((0,), (0,)), ((),...]
    dot_general x1 -> x0, matrix products: 30.1 us -> none  [per_device(): lax.dot_general(features_all, slope, (((0,), (0,)), ((), ())), preferred_...]
    all_to_all x0 -> x2, waiting for transfers between devices: none -> 12.1 us  [everyone(): lax.all_to_all(jnp.broadcast_to(vector[None, :], (count,) + vector.shape)...]
  transfers between devices with their start and end apart: 2 -> 56, of which waited for: 2 -> 22; matrix products, arithmetic and copies ran while one was open for 1% -> 6% of each run, Pallas kernels for 0% -> 21%
where the time goes in v1:
time: 269 us; the launch traced here: 268 us
  waiting for transfers between devices  97.8 us (36%)
  Pallas kernels  56.7 us (21%)
  starting transfers between devices  53.4 us (20%)
  other arithmetic  28.7 us (11%)
  local copies, waits for them, and re-layouts  20.4 us (8%)
  between operations  11.2 us (4%)
    ppermute x54, waiting for transfers between devices, send(): return lax.ppermute(value, BOTH, pairs)  85.7 us
    pallas_call x5, Pallas kernels, unit_partials(): pl.pallas_call(kernel, out_shape=(jax.ShapeDtypeStruct((rows, HALF), jnp....  56.7 us
    ppermute x54, starting transfers between devices, send(): return lax.ppermute(value, BOTH, pairs)  44.7 us
    all_to_all x2, waiting for transfers between devices, everyone(): lax.all_to_all(jnp.broadcast_to(vector[None, :], (count,) + vector.shape)...  12.1 us
    unnamed x74, local copies, waits for them, and re-layouts  11.7 us
    all_to_all x2, starting transfers between devices, everyone(): lax.all_to_all(jnp.broadcast_to(vector[None, :], (count,) + vector.shape)...  8.73 us
    convert_element_type x1, other arithmetic, gelu_slope(): (upstream.astype(jnp.float32) * (normal_cdf + value * density)).astype(jn...  6.12 us
  transfers between devices with their start and end apart: 56, of which 22 were waited for; matrix products, arithmetic and copies ran while one was open for 6% of the time, Pallas kernels for 21%

profile of v1, /device:TPU:0, one launch (start us, length us, event | category | flops | bytes accessed | tf_op | source)
XLA Modules:
  0.0 268.3 jit_solution(7912579190658415046)
XLA Ops:
  0.7 6.1 %fusion.14 = (bf16[1024,768]{1,0:T(8,128)(2,1)}, bf16[1024,768]{1,0:T(8,128)(2,1)S(1)}) fusion(bf16[1024,1536]{1,0:T(8,128)(2,1)} %param.9, s32[]{:T(128)S(6)} %select_n.91, bf16[1024,1536]{1,0:T(8,128)(2,1)} %param.10, s32[]{:T(128)S(6)} %select_n.90), kind=kLoop, calls=%fused_computation.28 | loop fusion | flops 18874368 | bytes 9437192 | tf_op jit(solution)/shard_map/convert_element_type | solution.py:51
  8.5 1.7 collective-permute-start.2
  10.2 1.5 collective-permute-start.14
  11.7 5.8 %collective-permute-done.2.refs_2_ = bf16[192,1024]{1,0:T(8,128)(2,1)S(1)} collective-permute-done((bf16[192,1024]{1,0:T(8,128)(2,1)S(1)}, bf16[192,1024]{1,0:T(8,128)(2,1)S(1)}, u32[]{:S(2)}, u32[]{:S(2)}) %collective-permute-start.2) | collective-permute-done | bytes 393248 | tf_op jit(solution)/shard_map/ppermute | solution.py:44
  17.9 1.5 collective-permute-start.5
  24.5 2.0 collective-permute-done.6.refs_6_
  26.5 1.9 collective-permute-done.17
  28.5 1.3 collective-permute-start.19
  31.2 6.2 %collective-permute-done.15 = bf16[192,1024]{1,0:T(8,128)(2,1)S(1)} collective-permute-done((bf16[192,1024]{1,0:T(8,128)(2,1)S(1)}, bf16[192,1024]{1,0:T(8,128)(2,1)S(1)}, u32[]{:S(2)}, u32[]{:S(2)}) %collective-permute-start.15) | collective-permute-done | bytes 393248 | tf_op jit(solution)/shard_map/ppermute | solution.py:44
  37.6 1.5 collective-permute-start.21
  39.2 1.4 collective-permute-start.33
  42.5 6.2 %shard_map.103 = (f32[192,768]{1,0:T(8,128)S(1)}, bf16[192,768]{1,0:T(8,128)(2,1)S(1)}, bf16[192,768]{1,0:T(8,128)(2,1)S(1)}, bf16[192,768]{1,0:T(8,128)(2,1)S(1)}) custom-call(s32[4]{0:T(128)S(1)} %and_select_fusion.order_ref, bf16[1024,768]{1,0:T(8,128)(2,1)S(1)} %get-tuple-element.50.own_ref, bf16[1024,768]{1,0:T(8,128)(2,1)} %collective-permute-done.other_ref, ...), custom_call_target="tpu_custom_call" | custom-call | flops 2415919104 | bytes 7766016 | tf_op jit(solution)/shard_map/pallas_call | solution.py:108
  48.8 2.0 collective-permute-start.8
  50.9 6.7 %collective-permute-done.8 = bf16[192,768]{1,0:T(8,128)(2,1)S(1)} collective-permute-done((bf16[192,768]{1,0:T(8,128)(2,1)S(1)}, bf16[192,768]{1,0:T(8,128)(2,1)S(1)}, u32[]{:S(2)}, u32[]{:S(2)}) %collective-permute-start.8) | collective-permute-done | bytes 294944 | tf_op jit(solution)/shard_map/ppermute | solution.py:44
  58.7 1.3 collective-permute-start.20
  60.2 1.3 collective-permute-start.29
  63.6 5.9 %collective-permute-done.9 = bf16[192,768]{1,0:T(8,128)(2,1)S(1)} collective-permute-done((bf16[192,768]{1,0:T(8,128)(2,1)S(1)}, bf16[192,768]{1,0:T(8,128)(2,1)S(1)}, u32[]{:S(2)}, u32[]{:S(2)}) %collective-permute-start.9) | collective-permute-done | bytes 294944 | tf_op jit(solution)/shard_map/ppermute | solution.py:44
  69.5 1.4 collective-permute-done.11.refs_0_
  72.0 7.4 %collective-permute-done.29.refs_0_ = bf16[4,96,1024]{2,1,0:T(8,128)(2,1)} collective-permute-done((bf16[4,96,1024]{2,1,0:T(8,128)(2,1)S(1)}, bf16[4,96,1024]{2,1,0:T(8,128)(2,1)}, u32[]{:S(2)}, u32[]{:S(2)}) %collective-permute-start.29) | collective-permute-done | bytes 786464 | tf_op jit(solution)/shard_map/ppermute | solution.py:44
  79.4 1.9 collective-permute-start.10
  81.6 6.5 %collective-permute-done.10 = bf16[192,768]{1,0:T(8,128)(2,1)S(1)} collective-permute-done((bf16[192,768]{1,0:T(8,128)(2,1)S(1)}, bf16[192,768]{1,0:T(8,128)(2,1)S(1)}, u32[]{:S(2)}, u32[]{:S(2)}) %collective-permute-start.10) | collective-permute-done | bytes 294944 | tf_op jit(solution)/shard_map/ppermute | solution.py:44
  89.1 1.3 collective-permute-start.23
  90.5 9.5 %shard_map.106 = (f32[192,768]{1,0:T(8,128)S(1)}, bf16[192,768]{1,0:T(8,128)(2,1)}, bf16[192,768]{1,0:T(8,128)(2,1)S(1)}, bf16[192,768]{1,0:T(8,128)(2,1)S(1)}) custom-call(s32[4]{0:T(128)S(1)} %and_select_fusion.order_ref, bf16[1024,768]{1,0:T(8,128)(2,1)S(1)} %get-tuple-element.50.own_ref, bf16[1024,768]{1,0:T(8,128)(2,1)} %collective-permute-done.other_ref, ...), custom_call_target="tpu_custom_call" | custom-call | flops 2415919104 | bytes 7766016 | tf_op jit(solution)/shard_map/pallas_call | solution.py:108
  101.6 8.6 %shard_map.107 = (f32[192,768]{1,0:T(8,128)S(1)}, bf16[192,768]{1,0:T(8,128)(2,1)}, bf16[192,768]{1,0:T(8,128)(2,1)S(1)}, bf16[192,768]{1,0:T(8,128)(2,1)S(1)}) custom-call(s32[4]{0:T(128)S(1)} %and_select_fusion.order_ref, bf16[1024,768]{1,0:T(8,128)(2,1)S(1)} %get-tuple-element.50.own_ref, bf16[1024,768]{1,0:T(8,128)(2,1)} %collective-permute-done.other_ref, ...), custom_call_target="tpu_custom_call" | custom-call | flops 2415919104 | bytes 7766016 | tf_op jit(solution)/shard_map/pallas_call | solution.py:108
  112.6 1.7 collective-permute-start.50
  114.3 1.7 collective-permute-start.30
  117.8 1.8 collective-permute-start.13
  129.4 1.7 collective-permute-start.45
  133.9 3.5 %collective-permute-done.45 = bf16[192,768]{1,0:T(8,128)(2,1)S(1)} collective-permute-done((bf16[192,768]{1,0:T(8,128)(2,1)S(1)}, bf16[192,768]{1,0:T(8,128)(2,1)S(1)}, u32[]{:S(2)}, u32[]{:S(2)}) %collective-permute-start.45) | collective-permute-done | bytes 294944 | tf_op jit(solution)/shard_map/ppermute | solution.py:44
  141.9 16.7 %shard_map.104 = (f32[480,768]{1,0:T(8,128)S(1)}, bf16[480,768]{1,0:T(8,128)(2,1)S(1)}, bf16[480,768]{1,0:T(8,128)(2,1)S(1)}, bf16[480,768]{1,0:T(8,128)(2,1)S(1)}) custom-call(s32[4]{0:T(128)S(1)} %and_select_fusion.order_ref, bf16[1024,768]{1,0:T(8,128)(2,1)S(1)} %get-tuple-element.50.own_ref, bf16[1024,768]{1,0:T(8,128)(2,1)} %collective-permute-done.other_ref, ...), custom_call_target="tpu_custom_call" | custom-call | flops 6039797760 | bytes 14696448 | tf_op jit(solution)/shard_map/pallas_call | solution.py:108
  159.2 15.7 %shard_map.105 = (f32[480,768]{1,0:T(8,128)S(1)}, bf16[480,768]{1,0:T(8,128)(2,1)S(1)}, bf16[480,768]{1,0:T(8,128)(2,1)S(1)}, bf16[480,768]{1,0:T(8,128)(2,1)S(1)}) custom-call(s32[4]{0:T(128)S(1)} %and_select_fusion.order_ref, bf16[1024,768]{1,0:T(8,128)(2,1)S(1)} %get-tuple-element.50.own_ref, bf16[1024,768]{1,0:T(8,128)(2,1)} %collective-permute-done.other_ref, ...), custom_call_target="tpu_custom_call" | custom-call | flops 6039797760 | bytes 14696448 | tf_op jit(solution)/shard_map/pallas_call | solution.py:108
  174.9 3.8 %collective-permute-start.38 = (bf16[480,768]{1,0:T(8,128)(2,1)S(1)}, bf16[480,768]{1,0:T(8,128)(2,1)S(1)}, u32[]{:S(2)}, u32[]{:S(2)}) collective-permute-start(bf16[480,768]{1,0:T(8,128)(2,1)S(1)} %get-tuple-element.34), channel_id=1, source_target_pairs={{0,2},{1,7},{2,4},{3,1},{4,6},{5,3},{6,0},{7,5},{8,10},{9,15},{10,... | collective-permute-start | bytes 2211848 | tf_op jit(solution)/shard_map/ppermute | solution.py:44
  179.8 7.8 %collective-permute-done.38 = bf16[480,768]{1,0:T(8,128)(2,1)S(1)} collective-permute-done((bf16[480,768]{1,0:T(8,128)(2,1)S(1)}, bf16[480,768]{1,0:T(8,128)(2,1)S(1)}, u32[]{:S(2)}, u32[]{:S(2)}) %collective-permute-start.38) | collective-permute-done | bytes 737312 | tf_op jit(solution)/shard_map/ppermute | solution.py:44
  187.8 2.5 collective-permute-start.39
  190.9 7.8 %collective-permute-done.27 = bf16[480,768]{1,0:T(8,128)(2,1)S(1)} collective-permute-done((bf16[480,768]{1,0:T(8,128)(2,1)S(1)}, bf16[480,768]{1,0:T(8,128)(2,1)S(1)}, u32[]{:S(2)}, u32[]{:S(2)}) %collective-permute-start.27) | collective-permute-done | bytes 737312 | tf_op jit(solution)/shard_map/ppermute | solution.py:44
  198.9 2.5 collective-permute-start.28
  201.5 5.1 %collective-permute-done.39 = bf16[480,768]{1,0:T(8,128)(2,1)S(1)} collective-permute-done((bf16[480,768]{1,0:T(8,128)(2,1)S(1)}, bf16[480,768]{1,0:T(8,128)(2,1)S(1)}, u32[]{:S(2)}, u32[]{:S(2)}) %collective-permute-start.39) | collective-permute-done | bytes 737312 | tf_op jit(solution)/shard_map/ppermute | solution.py:44
  206.8 2.5 collective-permute-start.40
  209.4 5.1 %collective-permute-done.28 = bf16[480,768]{1,0:T(8,128)(2,1)S(1)} collective-permute-done((bf16[480,768]{1,0:T(8,128)(2,1)S(1)}, bf16[480,768]{1,0:T(8,128)(2,1)S(1)}, u32[]{:S(2)}, u32[]{:S(2)}) %collective-permute-start.28) | collective-permute-done | bytes 737312 | tf_op jit(solution)/shard_map/ppermute | solution.py:44
  214.7 7.7 %collective-permute-done.40 = bf16[480,768]{1,0:T(8,128)(2,1)S(1)} collective-permute-done((bf16[480,768]{1,0:T(8,128)(2,1)S(1)}, bf16[480,768]{1,0:T(8,128)(2,1)S(1)}, u32[]{:S(2)}, u32[]{:S(2)}) %collective-permute-start.40) | collective-permute-done | bytes 737312 | tf_op jit(solution)/shard_map/ppermute | solution.py:44
  224.1 1.6 pad_maximum_fusion.2
  226.3 2.7 %multiply_reduce_fusion.1 = f32[1536]{0:T(1024)S(1)} fusion(f32[768,1536]{1,0:T(8,128)} %param.11), kind=kLoop, calls=%fused_computation.12 | loop fusion | flops 2357760 | bytes 4724736 | tf_op jit(solution)/shard_map/reduce_sum | solution.py:208
  230.3 4.3 %all-to-all-start = ((f32[8,1,2432]{2,1,0:T(1,128)}), f32[8,1,2432]{2,1,0:T(1,128)S(1)}, u32[]{:S(2)}, u32[]{:S(2)}) async-start(f32[8,1,2432]{2,1,0:T(1,128)} %broadcast_in_dim.11), calls=%async_computation | async-start | bytes 155648 | tf_op jit(solution)/shard_map/all_to_all | solution.py:136
  234.6 5.7 %all-to-all-done = f32[8,1,2432]{2,1,0:T(1,128)S(1)} async-done(((f32[8,1,2432]{2,1,0:T(1,128)}), f32[8,1,2432]{2,1,0:T(1,128)S(1)}, u32[]{:S(2)}, u32[]{:S(2)}) %all-to-all-start) | async-done | bytes 77856 | tf_op jit(solution)/shard_map/all_to_all | solution.py:136
  241.6 2.0 fusion.17
  247.7 4.4 %all-to-all-start.1 = ((f32[16,1,1024]{2,1,0:T(1,128)}), f32[16,1,1024]{2,1,0:T(1,128)S(1)}, u32[]{:S(2)}, u32[]{:S(2)}) async-start(f32[16,1,1024]{2,1,0:T(1,128)} %broadcast_in_dim.14), calls=%async_computation.1 | async-start | bytes 131072 | tf_op jit(solution)/shard_map/all_to_all | solution.py:136
  253.4 6.4 %all-to-all-done.1 = f32[16,1,1024]{2,1,0:T(1,128)S(1)} async-done(((f32[16,1,1024]{2,1,0:T(1,128)}), f32[16,1,1024]{2,1,0:T(1,128)S(1)}, u32[]{:S(2)}, u32[]{:S(2)}) %all-to-all-start.1) | async-done | bytes 65568 | tf_op jit(solution)/shard_map/all_to_all | solution.py:136
  263.0 5.3 %multiply_multiply_fusion = f32[768,1536]{1,0:T(8,128)} fusion(f32[768,768]{1,0:T(8,128)} %copy-done.29, f32[768,768]{1,0:T(8,128)} %copy-done.28, f32[1536]{0:T(1024)S(1)} %get-tuple-element.47, f32[768]{0:T(1024)S(1)} %get-tuple-element.45, f32[]{:T(128)} %bitcast.45, f32[1536]{0:T(1024)S(1)} %get-tuple-element.109), kind=kLoop, calls=%fused_computation.10 | loop fusion | flops 5898240 | bytes 9452548 | tf_op jit(solution)/shard_map/mul | solution.py:253
  (217 shorter events, 46.0 us)
Async XLA Ops:
  6.8 34.2 %collective-permute-start = (bf16[1024,768]{1,0:T(8,128)(2,1)}, bf16[1024,768]{1,0:T(8,128)(2,1)}, u32[]{:S(2)}, u32[]{:S(2)}) collective-permute-start(bf16[1024,768]{1,0:T(8,128)(2,1)} %get-tuple-element.49), channel_id=1, source_target_pairs={{0,1},{1,0},{2,3},{3,2},{4,5},{5,4},{6,7},{7,6},{8,9},{9,8},{10,11... | collective-permute-start | bytes 4718600 | tf_op jit(solution)/shard_map/ppermute | solution.py:44
  7.1 13.6 %collective-permute-start.1 = (bf16[384,1024]{1,0:T(8,128)(2,1)S(1)}, bf16[384,1024]{1,0:T(8,128)(2,1)}, u32[]{:S(2)}, u32[]{:S(2)}) collective-permute-start(bf16[384,1024]{1,0:T(8,128)(2,1)S(1)} %bitcast.90), channel_id=1, source_target_pairs={{0,1},{1,0},{2,3},{3,2},{4,5},{5,4},{6,7},{7,6},{8,9},{9,8},{10,11... | collective-permute-start | bytes 2359304 | tf_op jit(solution)/shard_map/ppermute | solution.py:44
  8.5 9.0 %collective-permute-start.2 = (bf16[192,1024]{1,0:T(8,128)(2,1)S(1)}, bf16[192,1024]{1,0:T(8,128)(2,1)S(1)}, u32[]{:S(2)}, u32[]{:S(2)}) collective-permute-start(bf16[192,1024]{1,0:T(8,128)(2,1)S(1)} %get-tuple-element.80.refs_0_), channel_id=1, source_target_pairs={{0,32},{1,97},{2,34},{3,99},{4,36},{5,101},{6,38},{7,103},{8,40},{... | collective-permute-start | bytes 1179656 | tf_op jit(solution)/shard_map/ppermute | solution.py:44
  10.2 9.3 %collective-permute-start.14 = (bf16[192,1024]{1,0:T(8,128)(2,1)}, bf16[192,1024]{1,0:T(8,128)(2,1)S(1)}, u32[]{:S(2)}, u32[]{:S(2)}) collective-permute-start(bf16[192,1024]{1,0:T(8,128)(2,1)} %get-tuple-element.79), channel_id=1, source_target_pairs={{0,8},{1,25},{2,10},{3,27},{4,12},{5,29},{6,14},{7,31},{8,16},{9,1... | collective-permute-start | bytes 1179656 | tf_op jit(solution)/shard_map/ppermute | solution.py:44
  17.5 9.0 %collective-permute-start.6 = (bf16[192,1024]{1,0:T(8,128)(2,1)S(1)}, bf16[192,1024]{1,0:T(8,128)(2,1)S(1)}, u32[]{:S(2)}, u32[]{:S(2)}) collective-permute-start(bf16[192,1024]{1,0:T(8,128)(2,1)S(1)} %collective-permute-done.2.refs_2_), channel_id=1, source_target_pairs={{0,32},{1,97},{2,34},{3,99},{4,36},{5,101},{6,38},{7,103},{8,40},{... | collective-permute-start | bytes 1179656 | tf_op jit(solution)/shard_map/ppermute | solution.py:44
  17.9 11.9 %collective-permute-start.5 = (bf16[192,1024]{1,0:T(8,128)(2,1)S(1)}, bf16[192,1024]{1,0:T(8,128)(2,1)S(1)}, u32[]{:S(2)}, u32[]{:S(2)}) collective-permute-start(bf16[192,1024]{1,0:T(8,128)(2,1)S(1)} %collective-permute-done.2.refs_2_), channel_id=1, source_target_pairs={{0,1},{1,0},{2,3},{3,2},{4,5},{5,4},{6,7},{7,6},{8,9},{9,8},{10,11... | collective-permute-start | bytes 1179656 | tf_op jit(solution)/shard_map/ppermute | solution.py:44
  19.5 9.0 %collective-permute-start.17 = (bf16[192,1024]{1,0:T(8,128)(2,1)S(1)}, bf16[192,1024]{1,0:T(8,128)(2,1)S(1)}, u32[]{:S(2)}, u32[]{:S(2)}) collective-permute-start(bf16[192,1024]{1,0:T(8,128)(2,1)S(1)} %collective-permute-done.14), channel_id=1, source_target_pairs={{0,8},{1,25},{2,10},{3,27},{4,12},{5,29},{6,14},{7,31},{8,16},{9,1... | collective-permute-start | bytes 1179656 | tf_op jit(solution)/shard_map/ppermute | solution.py:44
  26.5 14.1 %collective-permute-start.3 = (bf16[192,1024]{1,0:T(8,128)(2,1)S(1)}, bf16[192,1024]{1,0:T(8,128)(2,1)S(1)}, u32[]{:S(2)}, u32[]{:S(2)}) collective-permute-start(bf16[192,1024]{1,0:T(8,128)(2,1)S(1)} %get-tuple-element.78.refs_1_), channel_id=1, source_target_pairs={{0,32},{1,97},{2,34},{3,99},{4,36},{5,101},{6,38},{7,103},{8,40},{... | collective-permute-start | bytes 1179656 | tf_op jit(solution)/shard_map/ppermute | solution.py:44
  28.5 9.0 %collective-permute-start.15 = (bf16[192,1024]{1,0:T(8,128)(2,1)S(1)}, bf16[192,1024]{1,0:T(8,128)(2,1)S(1)}, u32[]{:S(2)}, u32[]{:S(2)}) collective-permute-start(bf16[192,1024]{1,0:T(8,128)(2,1)S(1)} %get-tuple-element.77), channel_id=1, source_target_pairs={{0,8},{1,25},{2,10},{3,27},{4,12},{5,29},{6,14},{7,31},{8,16},{9,1... | collective-permute-start | bytes 1179656 | tf_op jit(solution)/shard_map/ppermute | solution.py:44
  29.9 10.8 %collective-permute-start.7 = (bf16[192,1024]{1,0:T(8,128)(2,1)S(1)}, bf16[192,1024]{1,0:T(8,128)(2,1)S(1)}, u32[]{:S(2)}, u32[]{:S(2)}) collective-permute-start(bf16[192,1024]{1,0:T(8,128)(2,1)S(1)} %collective-permute-done.6.refs_6_), channel_id=1, source_target_pairs={{0,1},{1,0},{2,3},{3,2},{4,5},{5,4},{6,7},{7,6},{8,9},{9,8},{10,11... | collective-permute-start | bytes 1179656 | tf_op jit(solution)/shard_map/ppermute | solution.py:44
  37.6 21.1 %collective-permute-start.21 = (bf16[4,96,1024]{2,1,0:T(8,128)(2,1)S(1)}, bf16[4,96,1024]{2,1,0:T(8,128)(2,1)S(1)}, u32[]{:S(2)}, u32[]{:S(2)}) collective-permute-start(bf16[4,96,1024]{2,1,0:T(8,128)(2,1)S(1)} %pad_maximum_fusion.5.refs_3_), channel_id=1, source_target_pairs={{0,32},{1,97},{2,34},{3,99},{4,36},{5,101},{6,38},{7,103},{8,40},{... | collective-permute-start | bytes 2359304 | tf_op jit(solution)/shard_map/ppermute | solution.py:44
  39.2 21.0 %collective-permute-start.33 = (bf16[4,96,1024]{2,1,0:T(8,128)(2,1)S(1)}, bf16[4,96,1024]{2,1,0:T(8,128)(2,1)S(1)}, u32[]{:S(2)}, u32[]{:S(2)}) collective-permute-start(bf16[4,96,1024]{2,1,0:T(8,128)(2,1)S(1)} %pad_maximum_fusion.8.refs_3_), channel_id=1, source_target_pairs={{0,32},{1,97},{2,34},{3,99},{4,36},{5,101},{6,38},{7,103},{8,40},{... | collective-permute-start | bytes 2359304 | tf_op jit(solution)/shard_map/ppermute | solution.py:44
  40.8 20.8 %collective-permute-start.41 = (bf16[4,96,1024]{2,1,0:T(8,128)(2,1)S(1)}, bf16[4,96,1024]{2,1,0:T(8,128)(2,1)S(1)}, u32[]{:S(2)}, u32[]{:S(2)}) collective-permute-start(bf16[4,96,1024]{2,1,0:T(8,128)(2,1)S(1)} %pad_maximum_fusion.9), channel_id=1, source_target_pairs={{0,8},{1,25},{2,10},{3,27},{4,12},{5,29},{6,14},{7,31},{8,16},{9,1... | collective-permute-start | bytes 2359304 | tf_op jit(solution)/shard_map/ppermute | solution.py:44
  41.0 21.5 %collective-permute-start.47 = (bf16[4,96,1024]{2,1,0:T(8,128)(2,1)S(1)}, bf16[4,96,1024]{2,1,0:T(8,128)(2,1)S(1)}, u32[]{:S(2)}, u32[]{:S(2)}) collective-permute-start(bf16[4,96,1024]{2,1,0:T(8,128)(2,1)S(1)} %pad_maximum_fusion.10), channel_id=1, source_target_pairs={{0,8},{1,25},{2,10},{3,27},{4,12},{5,29},{6,14},{7,31},{8,16},{9,1... | collective-permute-start | bytes 2359304 | tf_op jit(solution)/shard_map/ppermute | solution.py:44
  57.6 13.3 %collective-permute-start.11 = (bf16[4,96,1024]{2,1,0:T(8,128)(2,1)S(1)}, bf16[4,96,1024]{2,1,0:T(8,128)(2,1)S(1)}, u32[]{:S(2)}, u32[]{:S(2)}) collective-permute-start(bf16[4,96,1024]{2,1,0:T(8,128)(2,1)S(1)} %pad_maximum_fusion.3), channel_id=1, source_target_pairs={{0,8},{1,25},{2,10},{3,27},{4,12},{5,29},{6,14},{7,31},{8,16},{9,1... | collective-permute-start | bytes 2359304 | tf_op jit(solution)/shard_map/ppermute | solution.py:44
  58.7 13.3 %collective-permute-start.20 = (bf16[4,96,1024]{2,1,0:T(8,128)(2,1)S(1)}, bf16[4,96,1024]{2,1,0:T(8,128)(2,1)S(1)}, u32[]{:S(2)}, u32[]{:S(2)}) collective-permute-start(bf16[4,96,1024]{2,1,0:T(8,128)(2,1)S(1)} %pad_maximum_fusion.4.refs_2_), channel_id=1, source_target_pairs={{0,32},{1,97},{2,34},{3,99},{4,36},{5,101},{6,38},{7,103},{8,40},{... | collective-permute-start | bytes 2359304 | tf_op jit(solution)/shard_map/ppermute | solution.py:44
  60.2 19.2 %collective-permute-start.29 = (bf16[4,96,1024]{2,1,0:T(8,128)(2,1)S(1)}, bf16[4,96,1024]{2,1,0:T(8,128)(2,1)}, u32[]{:S(2)}, u32[]{:S(2)}) collective-permute-start(bf16[4,96,1024]{2,1,0:T(8,128)(2,1)S(1)} %pad_maximum_fusion.6), channel_id=1, source_target_pairs={{0,8},{1,25},{2,10},{3,27},{4,12},{5,29},{6,14},{7,31},{8,16},{9,1... | collective-permute-start | bytes 2359304 | tf_op jit(solution)/shard_map/ppermute | solution.py:44
  62.5 18.9 %collective-permute-start.32 = (bf16[4,96,1024]{2,1,0:T(8,128)(2,1)S(1)}, bf16[4,96,1024]{2,1,0:T(8,128)(2,1)}, u32[]{:S(2)}, u32[]{:S(2)}) collective-permute-start(bf16[4,96,1024]{2,1,0:T(8,128)(2,1)S(1)} %pad_maximum_fusion.7.refs_2_), channel_id=1, source_target_pairs={{0,32},{1,97},{2,34},{3,99},{4,36},{5,101},{6,38},{7,103},{8,40},{... | collective-permute-start | bytes 2359304 | tf_op jit(solution)/shard_map/ppermute | solution.py:44
  69.5 18.7 %collective-permute-start.42 = (bf16[4,96,1024]{2,1,0:T(8,128)(2,1)S(1)}, bf16[4,96,1024]{2,1,0:T(8,128)(2,1)S(1)}, u32[]{:S(2)}, u32[]{:S(2)}) collective-permute-start(bf16[4,96,1024]{2,1,0:T(8,128)(2,1)S(1)} %collective-permute-done.41.refs_1_), channel_id=1, source_target_pairs={{0,1},{1,0},{2,3},{3,2},{4,5},{5,4},{6,7},{7,6},{8,9},{9,8},{10,11... | collective-permute-start | bytes 2359304 | tf_op jit(solution)/shard_map/ppermute | solution.py:44
  70.9 18.0 %collective-permute-start.48 = (bf16[4,96,1024]{2,1,0:T(8,128)(2,1)S(1)}, bf16[4,96,1024]{2,1,0:T(8,128)(2,1)S(1)}, u32[]{:S(2)}, u32[]{:S(2)}) collective-permute-start(bf16[4,96,1024]{2,1,0:T(8,128)(2,1)S(1)} %collective-permute-done.47.refs_1_), channel_id=1, source_target_pairs={{0,1},{1,0},{2,3},{3,2},{4,5},{5,4},{6,7},{7,6},{8,9},{9,8},{10,11... | collective-permute-start | bytes 2359304 | tf_op jit(solution)/shard_map/ppermute | solution.py:44
  71.9 17.2 %collective-permute-start.43 = (bf16[4,96,1024]{2,1,0:T(8,128)(2,1)S(1)}, bf16[4,96,1024]{2,1,0:T(8,128)(2,1)S(1)}, u32[]{:S(2)}, u32[]{:S(2)}) collective-permute-start(bf16[4,96,1024]{2,1,0:T(8,128)(2,1)S(1)} %collective-permute-done.11.refs_0_), channel_id=1, source_target_pairs={{0,1},{1,0},{2,3},{3,2},{4,5},{5,4},{6,7},{7,6},{8,9},{9,8},{10,11... | collective-permute-start | bytes 2359304 | tf_op jit(solution)/shard_map/ppermute | solution.py:44
  81.4 20.2 %collective-permute-start.49 = (bf16[4,96,1024]{2,1,0:T(8,128)(2,1)}, bf16[4,96,1024]{2,1,0:T(8,128)(2,1)S(1)}, u32[]{:S(2)}, u32[]{:S(2)}) collective-permute-start(bf16[4,96,1024]{2,1,0:T(8,128)(2,1)} %collective-permute-done.29.refs_0_), channel_id=1, source_target_pairs={{0,1},{1,0},{2,3},{3,2},{4,5},{5,4},{6,7},{7,6},{8,9},{9,8},{10,11... | collective-permute-start | bytes 2359304 | tf_op jit(solution)/shard_map/ppermute | solution.py:44
  88.2 23.6 %collective-permute-start.22 = (bf16[4,96,1024]{2,1,0:T(8,128)(2,1)S(1)}, bf16[4,96,1024]{2,1,0:T(8,128)(2,1)S(1)}, u32[]{:S(2)}, u32[]{:S(2)}) collective-permute-start(bf16[4,96,1024]{2,1,0:T(8,128)(2,1)S(1)} %collective-permute-done.21.refs_5_), channel_id=1, source_target_pairs={{0,1},{1,0},{2,3},{3,2},{4,5},{5,4},{6,7},{7,6},{8,9},{9,8},{10,11... | collective-permute-start | bytes 2359304 | tf_op jit(solution)/shard_map/ppermute | solution.py:44
  88.2 26.1 %collective-permute-start.12 = (bf16[4,96,1024]{2,1,0:T(8,128)(2,1)S(1)}, bf16[4,96,1024]{2,1,0:T(8,128)(2,1)}, u32[]{:S(2)}, u32[]{:S(2)}) collective-permute-start(bf16[4,96,1024]{2,1,0:T(8,128)(2,1)S(1)} %collective-permute-done.11.refs_0_), channel_id=1, source_target_pairs={{0,8},{1,25},{2,10},{3,27},{4,12},{5,29},{6,14},{7,31},{8,16},{9,1... | collective-permute-start | bytes 2359304 | tf_op jit(solution)/shard_map/ppermute | solution.py:44
  88.9 27.1 %collective-permute-start.24 = (bf16[4,96,1024]{2,1,0:T(8,128)(2,1)S(1)}, bf16[4,96,1024]{2,1,0:T(8,128)(2,1)S(1)}, u32[]{:S(2)}, u32[]{:S(2)}) collective-permute-start(bf16[4,96,1024]{2,1,0:T(8,128)(2,1)S(1)} %collective-permute-done.20.refs_4_), channel_id=1, source_target_pairs={{0,32},{1,97},{2,34},{3,99},{4,36},{5,101},{6,38},{7,103},{8,40},{... | collective-permute-start | bytes 2359304 | tf_op jit(solution)/shard_map/ppermute | solution.py:44
  89.1 27.0 %collective-permute-start.23 = (bf16[4,96,1024]{2,1,0:T(8,128)(2,1)S(1)}, bf16[4,96,1024]{2,1,0:T(8,128)(2,1)S(1)}, u32[]{:S(2)}, u32[]{:S(2)}) collective-permute-start(bf16[4,96,1024]{2,1,0:T(8,128)(2,1)S(1)} %collective-permute-done.20.refs_4_), channel_id=1, source_target_pairs={{0,1},{1,0},{2,3},{3,2},{4,5},{5,4},{6,7},{7,6},{8,9},{9,8},{10,11... | collective-permute-start | bytes 2359304 | tf_op jit(solution)/shard_map/ppermute | solution.py:44
  101.6 26.4 %collective-permute-start.44 = (bf16[192,768]{1,0:T(8,128)(2,1)}, bf16[192,768]{1,0:T(8,128)(2,1)}, u32[]{:S(2)}, u32[]{:S(2)}) collective-permute-start(bf16[192,768]{1,0:T(8,128)(2,1)} %get-tuple-element.38), channel_id=1, source_target_pairs={{0,2},{1,7},{2,4},{3,1},{4,6},{5,3},{6,0},{7,5},{8,10},{9,15},{10,... | collective-permute-start | bytes 884744 | tf_op jit(solution)/shard_map/ppermute | solution.py:44
  112.6 16.7 %collective-permute-start.50 = (bf16[192,768]{1,0:T(8,128)(2,1)}, bf16[192,768]{1,0:T(8,128)(2,1)}, u32[]{:S(2)}, u32[]{:S(2)}) collective-permute-start(bf16[192,768]{1,0:T(8,128)(2,1)} %get-tuple-element.42), channel_id=1, source_target_pairs={{0,2},{1,7},{2,4},{3,1},{4,6},{5,3},{6,0},{7,5},{8,10},{9,15},{10,... | collective-permute-start | bytes 884744 | tf_op jit(solution)/shard_map/ppermute | solution.py:44
  114.3 19.0 %collective-permute-start.30 = (bf16[4,96,1024]{2,1,0:T(8,128)(2,1)}, bf16[4,96,1024]{2,1,0:T(8,128)(2,1)}, u32[]{:S(2)}, u32[]{:S(2)}) collective-permute-start(bf16[4,96,1024]{2,1,0:T(8,128)(2,1)} %collective-permute-done.29.refs_0_), channel_id=1, source_target_pairs={{0,8},{1,25},{2,10},{3,27},{4,12},{5,29},{6,14},{7,31},{8,16},{9,1... | collective-permute-start | bytes 2359304 | tf_op jit(solution)/shard_map/ppermute | solution.py:44
  116.0 17.4 %collective-permute-start.36 = (bf16[4,96,1024]{2,1,0:T(8,128)(2,1)}, bf16[4,96,1024]{2,1,0:T(8,128)(2,1)}, u32[]{:S(2)}, u32[]{:S(2)}) collective-permute-start(bf16[4,96,1024]{2,1,0:T(8,128)(2,1)} %collective-permute-done.32.refs_4_), channel_id=1, source_target_pairs={{0,32},{1,97},{2,34},{3,99},{4,36},{5,101},{6,38},{7,103},{8,40},{... | collective-permute-start | bytes 2359304 | tf_op jit(solution)/shard_map/ppermute | solution.py:44
  117.8 19.6 %collective-permute-start.13 = (bf16[4,96,1024]{2,1,0:T(8,128)(2,1)}, bf16[4,96,1024]{2,1,0:T(8,128)(2,1)}, u32[]{:S(2)}, u32[]{:S(2)}) collective-permute-start(bf16[4,96,1024]{2,1,0:T(8,128)(2,1)} %collective-permute-done.12.refs_0_), channel_id=1, source_target_pairs={{0,1},{1,0},{2,3},{3,2},{4,5},{5,4},{6,7},{7,6},{8,9},{9,8},{10,11... | collective-permute-start | bytes 2359304 | tf_op jit(solution)/shard_map/ppermute | solution.py:44
  128.0 10.0 %collective-permute-start.25 = (bf16[4,96,1024]{2,1,0:T(8,128)(2,1)}, bf16[4,96,1024]{2,1,0:T(8,128)(2,1)S(1)}, u32[]{:S(2)}, u32[]{:S(2)}) collective-permute-start(bf16[4,96,1024]{2,1,0:T(8,128)(2,1)} %copy-done.24), channel_id=1, source_target_pairs={{0,1},{1,0},{2,3},{3,2},{4,5},{5,4},{6,7},{7,6},{8,9},{9,8},{10,11... | collective-permute-start | bytes 2359304 | tf_op jit(solution)/shard_map/ppermute | solution.py:44
  133.3 25.2 %collective-permute-start.34 = (bf16[4,96,1024]{2,1,0:T(8,128)(2,1)S(1)}, bf16[4,96,1024]{2,1,0:T(8,128)(2,1)S(1)}, u32[]{:S(2)}, u32[]{:S(2)}) collective-permute-start(bf16[4,96,1024]{2,1,0:T(8,128)(2,1)S(1)} %copy-done.17), channel_id=1, source_target_pairs={{0,1},{1,0},{2,3},{3,2},{4,5},{5,4},{6,7},{7,6},{8,9},{9,8},{10,11... | collective-permute-start | bytes 2359304 | tf_op jit(solution)/shard_map/ppermute | solution.py:44
  133.4 25.3 %collective-permute-start.35 = (bf16[4,96,1024]{2,1,0:T(8,128)(2,1)}, bf16[4,96,1024]{2,1,0:T(8,128)(2,1)S(1)}, u32[]{:S(2)}, u32[]{:S(2)}) collective-permute-start(bf16[4,96,1024]{2,1,0:T(8,128)(2,1)} %collective-permute-done.32.refs_4_), channel_id=1, source_target_pairs={{0,1},{1,0},{2,3},{3,2},{4,5},{5,4},{6,7},{7,6},{8,9},{9,8},{10,11... | collective-permute-start | bytes 2359304 | tf_op jit(solution)/shard_map/ppermute | solution.py:44
  137.4 21.8 %collective-permute-start.31 = (bf16[4,96,1024]{2,1,0:T(8,128)(2,1)}, bf16[4,96,1024]{2,1,0:T(8,128)(2,1)S(1)}, u32[]{:S(2)}, u32[]{:S(2)}) collective-permute-start(bf16[4,96,1024]{2,1,0:T(8,128)(2,1)} %collective-permute-done.30.refs_0_), channel_id=1, source_target_pairs={{0,1},{1,0},{2,3},{3,2},{4,5},{5,4},{6,7},{7,6},{8,9},{9,8},{10,11... | collective-permute-start | bytes 2359304 | tf_op jit(solution)/shard_map/ppermute | solution.py:44
  137.4 21.8 %collective-permute-start.37 = (bf16[4,96,1024]{2,1,0:T(8,128)(2,1)}, bf16[4,96,1024]{2,1,0:T(8,128)(2,1)S(1)}, u32[]{:S(2)}, u32[]{:S(2)}) collective-permute-start(bf16[4,96,1024]{2,1,0:T(8,128)(2,1)} %collective-permute-done.36.refs_8_), channel_id=1, source_target_pairs={{0,1},{1,0},{2,3},{3,2},{4,5},{5,4},{6,7},{7,6},{8,9},{9,8},{10,11... | collective-permute-start | bytes 2359304 | tf_op jit(solution)/shard_map/ppermute | solution.py:44
  138.0 40.7 %collective-permute-start.51 = (bf16[192,768]{1,0:T(8,128)(2,1)S(1)}, bf16[192,768]{1,0:T(8,128)(2,1)S(1)}, u32[]{:S(2)}, u32[]{:S(2)}) collective-permute-start(bf16[192,768]{1,0:T(8,128)(2,1)S(1)} %add_convert_fusion.5), channel_id=1, source_target_pairs={{0,2},{1,7},{2,4},{3,1},{4,6},{5,3},{6,0},{7,5},{8,10},{9,15},{10,... | collective-permute-start | bytes 884744 | tf_op jit(solution)/shard_map/ppermute | solution.py:44
  158.5 21.2 %collective-permute-start.46 = (bf16[192,768]{1,0:T(8,128)(2,1)S(1)}, bf16[192,768]{1,0:T(8,128)(2,1)S(1)}, u32[]{:S(2)}, u32[]{:S(2)}) collective-permute-start(bf16[192,768]{1,0:T(8,128)(2,1)S(1)} %add_convert_fusion.6), channel_id=1, source_target_pairs={{0,2},{1,7},{2,4},{3,1},{4,6},{5,3},{6,0},{7,5},{8,10},{9,15},{10,... | collective-permute-start | bytes 884744 | tf_op jit(solution)/shard_map/ppermute | solution.py:44
  158.7 20.5 %collective-permute-start.26 = (bf16[480,768]{1,0:T(8,128)(2,1)S(1)}, bf16[480,768]{1,0:T(8,128)(2,1)S(1)}, u32[]{:S(2)}, u32[]{:S(2)}) collective-permute-start(bf16[480,768]{1,0:T(8,128)(2,1)S(1)} %get-tuple-element.30), channel_id=1, source_target_pairs={{0,2},{1,7},{2,4},{3,1},{4,6},{5,3},{6,0},{7,5},{8,10},{9,15},{10,... | collective-permute-start | bytes 2211848 | tf_op jit(solution)/shard_map/ppermute | solution.py:44
  174.9 12.7 %collective-permute-start.38 = (bf16[480,768]{1,0:T(8,128)(2,1)S(1)}, bf16[480,768]{1,0:T(8,128)(2,1)S(1)}, u32[]{:S(2)}, u32[]{:S(2)}) collective-permute-start(bf16[480,768]{1,0:T(8,128)(2,1)S(1)} %get-tuple-element.34), channel_id=1, source_target_pairs={{0,2},{1,7},{2,4},{3,1},{4,6},{5,3},{6,0},{7,5},{8,10},{9,15},{10,... | collective-permute-start | bytes 2211848 | tf_op jit(solution)/shard_map/ppermute | solution.py:44
  178.7 12.1 %collective-permute-start.52 = (bf16[192,768]{1,0:T(8,128)(2,1)S(1)}, bf16[192,768]{1,0:T(8,128)(2,1)S(1)}, u32[]{:S(2)}, u32[]{:S(2)}) collective-permute-start(bf16[192,768]{1,0:T(8,128)(2,1)S(1)} %add_convert_fusion.4), channel_id=1, source_target_pairs={{0,2},{1,7},{2,4},{3,1},{4,6},{5,3},{6,0},{7,5},{8,10},{9,15},{10,... | collective-permute-start | bytes 884744 | tf_op jit(solution)/shard_map/ppermute | solution.py:44
  179.4 19.3 %collective-permute-start.27 = (bf16[480,768]{1,0:T(8,128)(2,1)S(1)}, bf16[480,768]{1,0:T(8,128)(2,1)S(1)}, u32[]{:S(2)}, u32[]{:S(2)}) collective-permute-start(bf16[480,768]{1,0:T(8,128)(2,1)S(1)} %add_convert_fusion.3), channel_id=1, source_target_pairs={{0,2},{1,7},{2,4},{3,1},{4,6},{5,3},{6,0},{7,5},{8,10},{9,15},{10,... | collective-permute-start | bytes 2211848 | tf_op jit(solution)/shard_map/ppermute | solution.py:44
  187.8 18.8 %collective-permute-start.39 = (bf16[480,768]{1,0:T(8,128)(2,1)S(1)}, bf16[480,768]{1,0:T(8,128)(2,1)S(1)}, u32[]{:S(2)}, u32[]{:S(2)}) collective-permute-start(bf16[480,768]{1,0:T(8,128)(2,1)S(1)} %add_convert_fusion.1), channel_id=1, source_target_pairs={{0,2},{1,7},{2,4},{3,1},{4,6},{5,3},{6,0},{7,5},{8,10},{9,15},{10,... | collective-permute-start | bytes 2211848 | tf_op jit(solution)/shard_map/ppermute | solution.py:44
  198.9 15.6 %collective-permute-start.28 = (bf16[480,768]{1,0:T(8,128)(2,1)S(1)}, bf16[480,768]{1,0:T(8,128)(2,1)S(1)}, u32[]{:S(2)}, u32[]{:S(2)}) collective-permute-start(bf16[480,768]{1,0:T(8,128)(2,1)S(1)} %add_convert_fusion.2), channel_id=1, source_target_pairs={{0,2},{1,7},{2,4},{3,1},{4,6},{5,3},{6,0},{7,5},{8,10},{9,15},{10,... | collective-permute-start | bytes 2211848 | tf_op jit(solution)/shard_map/ppermute | solution.py:44
  206.8 15.6 %collective-permute-start.40 = (bf16[480,768]{1,0:T(8,128)(2,1)S(1)}, bf16[480,768]{1,0:T(8,128)(2,1)S(1)}, u32[]{:S(2)}, u32[]{:S(2)}) collective-permute-start(bf16[480,768]{1,0:T(8,128)(2,1)S(1)} %add_convert_fusion), channel_id=1, source_target_pairs={{0,2},{1,7},{2,4},{3,1},{4,6},{5,3},{6,0},{7,5},{8,10},{9,15},{10,... | collective-permute-start | bytes 2211848 | tf_op jit(solution)/shard_map/ppermute | solution.py:44
  225.7 16.0 %collective-permute-start.53 = (f32[768,768]{1,0:T(8,128)}, f32[768,768]{1,0:T(8,128)}, u32[]{:S(2)}, u32[]{:S(2)}) collective-permute-start(f32[768,768]{1,0:T(8,128)} %pad_maximum_fusion.2), channel_id=1, source_target_pairs={{0,1},{1,0},{2,3},{3,2},{4,5},{5,4},{6,7},{7,6},{8,9},{9,8},{10,11... | collective-permute-start | bytes 7077896 | tf_op jit(solution)/shard_map/ppermute | solution.py:44
  230.3 10.0 %all-to-all-start = ((f32[8,1,2432]{2,1,0:T(1,128)}), f32[8,1,2432]{2,1,0:T(1,128)S(1)}, u32[]{:S(2)}, u32[]{:S(2)}) async-start(f32[8,1,2432]{2,1,0:T(1,128)} %broadcast_in_dim.11), calls=%async_computation | async-start | bytes 155648 | tf_op jit(solution)/shard_map/all_to_all | solution.py:136
  247.7 12.1 %all-to-all-start.1 = ((f32[16,1,1024]{2,1,0:T(1,128)}), f32[16,1,1024]{2,1,0:T(1,128)S(1)}, u32[]{:S(2)}, u32[]{:S(2)}) async-start(f32[16,1,1024]{2,1,0:T(1,128)} %broadcast_in_dim.14), calls=%async_computation.1 | async-start | bytes 131072 | tf_op jit(solution)/shard_map/all_to_all | solution.py:136
  (44 other events, 357.7 us)
